TPU v7x, 32 devices: a whole 2x2x4 slice. The times are simulated.
32 devices in a mesh: parts: 2 (over x), mp: 16 (over z, y, core).
Axes of the slice: x: 2, y: 2, z: 4, core: 2. Of those that a mesh axis runs over, the one named last changes fastest.
Arguments:
- probes: float32 [32, 262144], P(None, ('parts', 'mp')), parts along dimension 1, may hold values from -6 to 6
- illumination: float32 [4, 262144], P(None, ('parts', 'mp')), parts along dimension 1, may hold values from 1 to 90, as said below
- damping: float32 [262144], P(('parts', 'mp')), parts along dimension 0, may hold values from 0.5 to 2
- wavelets: float32 [8, 513], P('parts'), parts along dimension 0, may hold values from -0.25 to 0.25
Outputs:
- basis: float32 [32, 262144], P(None, ('parts', 'mp')), parts along dimension 1
- r_factor: float32 [64, 32], P('parts'), parts along dimension 0
There are 2 independent parts, one for each index of `parts`. A program takes and returns all parts, laid end to end along the dimension named above; each array names one. Nothing has to cross between parts.
Inputs may be any that keep to these rules, and one draw needn't show every extreme that they name: `illumination`: positive data weights.
All inputs are finite; a program needn't handle non-finite values.
Results may differ from a plain program's by a relative error of at most 0.0001.
Values sent between devices are 32-bit elements; how exact they have to be, the bound alone decides.
A program may use at most 64 MiB of HBM per device.

v0:
```python
import functools

import jax
import jax.numpy as jnp
from jax import lax
from jax.experimental import pallas as pl
from jax.experimental.pallas import tpu as pltpu
from jax.sharding import PartitionSpec as P

W = 256
LANES = 128
MESH = pl.DeviceIdType.MESH
F32 = jnp.float32
BF16 = jnp.bfloat16
EXACT = lax.Precision.HIGHEST


def split(value):
    high = value.astype(BF16)
    return high, (value - high.astype(F32)).astype(BF16)


def iota(shape, dim):
    return lax.broadcasted_iota(jnp.int32, shape, dim)


def store_band(taps, last, high_ref, low_ref, shot):
    top = pltpu.roll(
        jnp.broadcast_to(taps, (LANES, 2 * W)), 0, 1, stride=1, stride_axis=0
    )
    bottom = jnp.concatenate([top[:, 2 * W - LANES :], top[:, : 2 * W - LANES]], axis=1)
    turned = jnp.concatenate([top, bottom], axis=0)
    edge = turned[:, :W]
    row, col = iota((W, W), 0), iota((W, W), 1)
    first = jnp.where(col < row, edge, jnp.where(col == row, last, 0.0))
    third = jnp.where(col >= row, edge, 0.0)
    for offset, tile in enumerate((first, turned[:, W:], third)):
        high, low = split(tile)
        rows = slice(offset * W, (offset + 1) * W)
        high_ref[shot, rows, :] = high
        low_ref[shot, rows, :] = low


def gram_of(high_ref, low_ref, start, block_count, rows):
    group = 8 * rows
    total = None
    for g in range(block_count // 8):
        at = slice(start + g * group, start + (g + 1) * group)
        high, low = high_ref[at, :], low_ref[at, :]
        left = jnp.concatenate([high, high, low], axis=1)
        right = jnp.concatenate([high, low, high], axis=1)
        term = lax.dot_general(
            left, right, (((1,), (1,)), ((), ())), preferred_element_type=F32
        )
        total = term if total is None else total + term
    same = iota((group, group), 0) // rows == iota((group, group), 1) // rows
    total = jnp.where(same, total, 0.0)
    folded = total[:rows]
    for i in range(1, 8):
        folded = folded + total[i * rows : (i + 1) * rows]
    folded = folded[:, :LANES] + folded[:, LANES:]
    folded = folded + pltpu.roll(folded, 64, 1)
    folded = folded + pltpu.roll(folded, 32, 1)
    lane = iota((8, LANES), 1) // 32
    packed = folded[:8]
    for i in range(1, 4):
        packed = jnp.where(lane == i, folded[8 * i : 8 * i + 8], packed)
    return packed


def unpack(packed):
    slabs = [packed] + [pltpu.roll(packed, LANES - 32 * i, 1) for i in range(1, 4)]
    return jnp.concatenate(slabs, axis=0)


def factor(gram, rows):
    row, lane = iota((rows, LANES), 0), iota((rows, LANES), 1)
    work = jnp.where(lane < rows, gram, jnp.where(lane == row + rows, 1.0, 0.0))
    unit = jnp.zeros((rows, LANES), F32)
    for k in range(rows):
        pivot_row = work[k : k + 1, :]
        ratio = work[:, k : k + 1] * (1.0 / work[k : k + 1, k : k + 1])
        unit = jnp.where((lane == k) & (row >= k), ratio, unit)
        work = work - jnp.where(row > k, ratio, 0.0) * pivot_row
    diagonal = jnp.where(lane == row, work, 0.0)
    down = jnp.sum(diagonal, axis=1, keepdims=True)
    along = jnp.sum(diagonal, axis=0, keepdims=True)
    lower = unit * jnp.sqrt(along)
    inverse = pltpu.roll(work, LANES - rows, 1) / jnp.sqrt(down)
    return lower[:, :rows], inverse[:, :rows]


def forward_stage(count, chunks, rows, src, weights, dst, light_ref, light_at, shots):
    step = count // chunks
    size = step * rows

    def chunk(c, carry):
        start = c * step
        at = pl.multiple_of(start * rows, rows)
        highs = [src[0][pl.ds(at + o * rows, size), :] for o in range(3)]
        lows = [src[1][pl.ds(at + o * rows, size), :] for o in range(3)]
        left = jnp.concatenate(highs + lows + highs, axis=1)
        for s in range(shots):
            wh, wl = weights[0][s], weights[1][s]
            right = jnp.concatenate([wh, wh, wl], axis=0)
            acc = jnp.dot(left, right, preferred_element_type=F32)
            light = jnp.concatenate(
                [
                    jnp.broadcast_to(light_ref[start + light_at + j, s : s + 1, :], (rows, W))
                    for j in range(step)
                ],
                axis=0,
            )
            high, low = split(acc * light)
            dst[0][s, pl.ds(at, size), :] = high
            dst[1][s, pl.ds(at, size), :] = low
        return carry

    lax.fori_loop(0, chunks, chunk, 0)


def adjoint_stage(count, chunks, rows, src, weights, dst, same, damp_ref, damp_at, shots):
    step = count // chunks
    size = step * rows

    def chunk(c, carry):
        start = c * step
        at = pl.multiple_of(start * rows, rows)
        acc = None
        for s in range(shots):
            highs = [src[0][s, pl.ds(at + o * rows, size), :] for o in range(3)]
            lows = [src[1][s, pl.ds(at + o * rows, size), :] for o in range(3)]
            wh, wl = weights[0][s], weights[1][s]
            left = jnp.concatenate(highs + lows + highs, axis=1)
            right = jnp.concatenate([wh, wh, wl], axis=0)
            term = jnp.dot(left, right, preferred_element_type=F32)
            acc = term if acc is None else acc + term
        own = pl.ds(at + 2 * rows, size)
        value = same[0][own, :].astype(F32) + same[1][own, :].astype(F32)
        damp = jnp.concatenate(
            [
                jnp.broadcast_to(damp_ref[start + damp_at + j], (rows, W))
                for j in range(step)
            ],
            axis=0,
        )
        high, low = split(acc * (1.0 / shots) + damp * value)
        dst[0][pl.ds(at, size), :] = high
        dst[1][pl.ds(at, size), :] = low
        return carry

    lax.fori_loop(0, chunks, chunk, 0)


def kernel(
    n, nb, rows, shots,
    probes, illum, damp, wav, basis, r_out,
    p_left, p_right, l_left, l_right, d_left, d_right,
    xh, xl, rh, rl, yh, yl, zh, zl, fh, fl, ah, al,
    light, damps, g_own, g_all, halo_send, halo_recv, g_send, g_recv,
):
    me = lax.axis_index("mp")
    cells = nb * W

    barrier = pltpu.get_barrier_semaphore()

    def greet(d, carry):
        pl.semaphore_signal(
            barrier, inc=1, device_id={"mp": lax.rem(me + d, n)}, device_id_type=MESH
        )
        return carry

    lax.fori_loop(1, n, greet, 0)

    def put(b, value):
        high, low = split(value)
        xh[b * rows : (b + 1) * rows, :] = high
        xl[b * rows : (b + 1) * rows, :] = low

    for b in range(nb):
        put(b + 4, probes[:, b * W : (b + 1) * W])
        light[b + 3] = illum[:, b * W : (b + 1) * W]
        damps[b + 2] = damp[:, b * W : (b + 1) * W]

    pl.semaphore_wait(barrier, n - 1)

    def halo(src, depth, to_right, dst, slot):
        at = pl.ds(cells - depth * W, depth * W) if to_right else pl.ds(0, depth * W)
        peer = lax.rem(me + 1, n) if to_right else lax.rem(me + n - 1, n)
        return pltpu.make_async_remote_copy(
            src_ref=src.at[:, at], dst_ref=dst,
            send_sem=halo_send.at[slot], recv_sem=halo_recv.at[slot],
            device_id={"mp": peer}, device_id_type=MESH,
        )

    rightward = [halo(probes, 4, True, p_left, 0), halo(illum, 3, True, l_left, 1),
                 halo(damp, 2, True, d_left, 2)]
    leftward = [halo(probes, 4, False, p_right, 3), halo(illum, 3, False, l_right, 4),
                halo(damp, 2, False, d_right, 5)]

    @pl.when(me < n - 1)
    def _():
        for copy in rightward:
            copy.start()

    @pl.when(me > 0)
    def _():
        for copy in leftward:
            copy.start()

    taps = wav[...]
    halves = jnp.concatenate([taps[:, :W], taps[:, W : 2 * W]], axis=0)
    turn = jnp.where(iota((W, W), 0) + iota((W, W), 1) == W - 1, 1.0, 0.0)
    flipped = jnp.dot(halves, turn, precision=EXACT, preferred_element_type=F32)
    back = jnp.concatenate([flipped[shots:], flipped[:shots]], axis=1)
    back = pltpu.roll(back, 1, 1)
    final = taps[:, 2 * W : 2 * W + 1]
    back = jnp.where(iota((shots, 2 * W), 1) == 0, final, back)
    for s in range(shots):
        store_band(taps[s : s + 1, : 2 * W], final[s : s + 1], fh, fl, s)
        store_band(back[s : s + 1], taps[s : s + 1, 0:1], ah, al, s)

    @pl.when(me > 0)
    def _():
        for copy in rightward:
            copy.wait_recv()

    @pl.when(me == 0)
    def _():
        p_left[...] = jnp.zeros_like(p_left)
        l_left[...] = jnp.zeros_like(l_left)
        d_left[...] = jnp.zeros_like(d_left)

    @pl.when(me < n - 1)
    def _():
        for copy in leftward:
            copy.wait_recv()

    @pl.when(me == n - 1)
    def _():
        p_right[...] = jnp.zeros_like(p_right)
        l_right[...] = jnp.zeros_like(l_right)
        d_right[...] = jnp.zeros_like(d_right)

    for b in range(4):
        put(b, p_left[:, b * W : (b + 1) * W])
        put(nb + 4 + b, p_right[:, b * W : (b + 1) * W])
    for b in range(3):
        light[b] = l_left[:, b * W : (b + 1) * W]
        light[nb + 3 + b] = l_right[:, b * W : (b + 1) * W]
    for b in range(2):
        damps[b] = d_left[:, b * W : (b + 1) * W]
        damps[nb + 2 + b] = d_right[:, b * W : (b + 1) * W]

    def send_gram(k, packed):
        g_own[k] = packed
        g_all[k, me] = packed

        def send(d, carry):
            gram_copy(k, d).start()
            return carry

        lax.fori_loop(1, n, send, 0)

    def gram_copy(k, d):
        return pltpu.make_async_remote_copy(
            src_ref=g_own.at[k], dst_ref=g_all.at[k, me],
            send_sem=g_send.at[k, d], recv_sem=g_recv.at[k, me],
            device_id={"mp": lax.rem(me + d, n)}, device_id_type=MESH,
        )

    def gathered(k):
        def arrive(d, carry):
            peer = lax.rem(me + d, n)
            pltpu.make_async_remote_copy(
                src_ref=g_own.at[k], dst_ref=g_all.at[k, peer],
                send_sem=g_send.at[k, d], recv_sem=g_recv.at[k, peer],
                device_id={"mp": peer}, device_id_type=MESH,
            ).wait_recv()
            return carry

        lax.fori_loop(1, n, arrive, 0)
        return unpack(jnp.sum(g_all[k], axis=0)) / (n * cells)

    forward_stage(nb + 6, 2, rows, (xh, xl), (fh, fl), (rh, rl), light, 0, shots)
    adjoint_stage(nb + 4, 2, rows, (rh, rl), (ah, al), (yh, yl), (xh, xl), damps, 0, shots)

    @pl.when(me == 0)
    def _():
        for ref in (yh, yl):
            ref[: 2 * rows, :] = jnp.zeros((2 * rows, W), BF16)

    @pl.when(me == n - 1)
    def _():
        for ref in (yh, yl):
            ref[(nb + 2) * rows :, :] = jnp.zeros((2 * rows, W), BF16)

    send_gram(0, gram_of(yh, yl, 2 * rows, nb, rows))
    forward_stage(nb + 2, 2, rows, (yh, yl), (fh, fl), (rh, rl), light, 2, shots)
    adjoint_stage(nb, 2, rows, (rh, rl), (ah, al), (zh, zl), (yh, yl), damps, 2, shots)
    send_gram(1, gram_of(zh, zl, 0, nb, rows))

    _, inverse = factor(gathered(0), rows)
    second = gathered(1)[:, :rows]
    second = jnp.dot(inverse, second, precision=EXACT, preferred_element_type=F32)
    second = lax.dot_general(
        second, inverse, (((1,), (1,)), ((), ())), precision=EXACT, preferred_element_type=F32
    )
    second = jnp.concatenate([second, jnp.zeros((rows, LANES - rows), F32)], axis=1)
    lower, inverse_2 = factor(second, rows)
    r_out[...] = lower
    both = jnp.dot(inverse_2, inverse, precision=EXACT, preferred_element_type=F32)
    wide = jnp.concatenate([both] * 8, axis=1)
    tall = jnp.concatenate([wide] * 8, axis=0)
    group = 8 * rows
    same = iota((group, group), 0) // rows == iota((group, group), 1) // rows
    high, low = split(jnp.where(same, tall, 0.0))
    left = jnp.concatenate([high, high, low], axis=1)
    for g in range(nb // 8):
        at = slice(g * group, (g + 1) * group)
        right = jnp.concatenate([zh[at, :], zl[at, :], zh[at, :]], axis=0)
        out = jnp.dot(left, right, preferred_element_type=F32)
        for i in range(8):
            b = g * 8 + i
            basis[:, b * W : (b + 1) * W] = out[i * rows : (i + 1) * rows]

    @pl.when(me < n - 1)
    def _():
        for copy in rightward:
            copy.wait_send()

    @pl.when(me > 0)
    def _():
        for copy in leftward:
            copy.wait_send()

    def sent(d, carry):
        gram_copy(0, d).wait_send()
        gram_copy(1, d).wait_send()
        return carry

    lax.fori_loop(1, n, sent, 0)


def per_device(n, probes, illumination, damping, wavelets):
    rows, cells = probes.shape
    shots = illumination.shape[0]
    nb = cells // W
    damping = damping.reshape(1, cells)
    vmem = pltpu.VMEM
    scratch = [
        vmem((rows, 4 * W), F32), vmem((rows, 4 * W), F32),
        vmem((shots, 3 * W), F32), vmem((shots, 3 * W), F32),
        vmem((1, 2 * W), F32), vmem((1, 2 * W), F32),
    ]
    scratch += [vmem(((nb + 8) * rows, W), BF16)] * 2
    scratch += [vmem((shots, (nb + 6) * rows, W), BF16)] * 2
    scratch += [vmem(((nb + 4) * rows, W), BF16)] * 2
    scratch += [vmem((nb * rows, W), BF16)] * 2
    scratch += [vmem((shots, 3 * W, W), BF16)] * 4
    scratch += [
        vmem((nb + 6, shots, W), F32), vmem((nb + 4, 1, W), F32),
        vmem((2, 8, LANES), F32), vmem((2, n, 8, LANES), F32),
        pltpu.SemaphoreType.DMA((6,)), pltpu.SemaphoreType.DMA((6,)),
        pltpu.SemaphoreType.DMA((2, n)), pltpu.SemaphoreType.DMA((2, n)),
    ]
    return pl.pallas_call(
        functools.partial(kernel, n, nb, rows, shots),
        out_shape=(
            jax.ShapeDtypeStruct((rows, cells), F32),
            jax.ShapeDtypeStruct((rows, rows), F32),
        ),
        in_specs=[pl.BlockSpec(memory_space=vmem)] * 4,
        out_specs=(pl.BlockSpec(memory_space=vmem), pl.BlockSpec(memory_space=vmem)),
        scratch_shapes=scratch,
        compiler_params=pltpu.CompilerParams(
            collective_id=0, has_side_effects=True, vmem_limit_bytes=48 * 2**20
        ),
    )(probes, illumination, damping, wavelets)


def solution(mesh):
    in_specs = (
        P(None, ("parts", "mp")),
        P(None, ("parts", "mp")),
        P(("parts", "mp")),
        P("parts", None),
    )
    out_specs = (P(None, ("parts", "mp")), P("parts", None))
    return jax.shard_map(
        functools.partial(per_device, mesh.shape["mp"]),
        mesh=mesh, in_specs=in_specs, out_specs=out_specs, check_vma=False,
    )
```

profile of v0, /device:TPU:0, one launch (start us, length us, event | category | flops | bytes accessed | tf_op | source)
XLA Modules:
  0.0 49.6 jit_solution(7547708281235007049)
XLA Ops:
  0.6 0.0 copy-start
  0.6 1.2 %copy-done = f32[32,8192]{1,0:T(8,128)S(1)} copy-done((f32[32,8192]{1,0:T(8,128)S(1)}, f32[32,8192]{1,0:T(8,128)}, u32[]{:S(2)}) %copy-start) | copy-done | bytes 1048600
  1.9 0.0 copy-start.1
  1.9 0.9 %copy-done.1 = f32[4,8192]{1,0:T(4,128)S(1)} copy-done((f32[4,8192]{1,0:T(4,128)S(1)}, f32[4,8192]{1,0:T(4,128)}, u32[]{:S(2)}) %copy-start.1) | copy-done | bytes 131096
  2.8 0.0 copy-start.2
  2.8 0.8 %copy-done.2 = f32[8192]{0:T(1024)S(1)} copy-done((f32[8192]{0:T(1024)S(1)}, f32[8192]{0:T(1024)}, u32[]{:S(2)}) %copy-start.2) | copy-done | bytes 32792
  3.5 0.0 copy-start.3
  3.5 0.7 %copy-done.3 = f32[4,513]{1,0:T(4,128)S(1)} copy-done((f32[4,513]{1,0:T(4,128)S(1)}, f32[4,513]{1,0:T(4,128)}, u32[]{:S(2)}) %copy-start.3) | copy-done | bytes 8232
  4.2 43.8 %shard_map.59 = (f32[32,8192]{1,0:T(8,128)S(1)}, f32[32,32]{1,0:T(8,128)S(1)}) custom-call(f32[32,8192]{1,0:T(8,128)S(1)} %copy-done, f32[4,8192]{1,0:T(4,128)S(1)} %copy-done.1, f32[1,8192]{1,0:T(1,128)S(1)} %bitcast.1, f32[4,513]{1,0:T(4,128)S(1)} %copy-done.3), custom_call_target="tpu_custom_call" | custom-call | tf_op jit(solution)/shard_map/pallas_call | solution.py:367
  48.0 1.0 %copy.8 = f32[32,8192]{1,0:T(8,128)} copy(f32[32,8192]{1,0:T(8,128)S(1)} %get-tuple-element.4) | data formatting | bytes 2097152
  49.0 0.6 %copy.9 = f32[32,32]{1,0:T(8,128)} copy(f32[32,32]{1,0:T(8,128)S(1)} %get-tuple-element.5) | data formatting | bytes 8192
Async XLA Ops:
  0.6 1.2 %copy-start = (f32[32,8192]{1,0:T(8,128)S(1)}, f32[32,8192]{1,0:T(8,128)}, u32[]{:S(2)}) copy-start(f32[32,8192]{1,0:T(8,128)} %probes.1) | copy-start | bytes 3145732
  1.9 0.9 %copy-start.1 = (f32[4,8192]{1,0:T(4,128)S(1)}, f32[4,8192]{1,0:T(4,128)}, u32[]{:S(2)}) copy-start(f32[4,8192]{1,0:T(4,128)} %illum.1) | copy-start | bytes 393220
  2.8 0.8 %copy-start.2 = (f32[8192]{0:T(1024)S(1)}, f32[8192]{0:T(1024)}, u32[]{:S(2)}) copy-start(f32[8192]{0:T(1024)} %param.6) | copy-start | bytes 98308
  3.5 0.7 %copy-start.3 = (f32[4,513]{1,0:T(4,128)S(1)}, f32[4,513]{1,0:T(4,128)}, u32[]{:S(2)}) copy-start(f32[4,513]{1,0:T(4,128)} %wav.1) | copy-start | bytes 24628
where the time goes:
time: 49.9 us; the launch traced here: 49.6 us
  Pallas kernels  43.8 us (88%)
  local copies, waits for them, and re-layouts  5.16 us (10%)
  between operations  0.65 us (1%)
    pallas_call x1, Pallas kernels, per_device(): pl.pallas_call(functools.partial(kernel, n, nb, rows, shots), out_shape=(...  43.8 us
    unnamed x10, local copies, waits for them, and re-layouts  5.16 us

commit v1 on v0

--- a/solution.py
+++ b/solution.py
@@ -90,30 +90,39 @@
     return lower[:, :rows], inverse[:, :rows]
 
 
-def forward_stage(count, chunks, rows, src, weights, dst, light_ref, light_at, shots):
+def forward_blocks(starts, step, rows, src, weights, dst, light_ref, light_at, shots):
+    size = step * rows
+    ats = [s * rows if isinstance(s, int) else pl.multiple_of(s * rows, rows) for s in starts]
+
+    def tall(ref, o):
+        return jnp.concatenate([ref[pl.ds(at + o * rows, size), :] for at in ats], axis=0)
+
+    highs = [tall(src[0], o) for o in range(3)]
+    lows = [tall(src[1], o) for o in range(3)]
+    left = jnp.concatenate(highs + lows + highs, axis=1)
+    for s in range(shots):
+        wh, wl = weights[0][s], weights[1][s]
+        right = jnp.concatenate([wh, wh, wl], axis=0)
+        acc = jnp.dot(left, right, preferred_element_type=F32)
+        light = jnp.concatenate(
+            [
+                jnp.broadcast_to(light_ref[start + light_at + j, s : s + 1, :], (rows, W))
+                for start in starts
+                for j in range(step)
+            ],
+            axis=0,
+        )
+        high, low = split(acc * light)
+        for i, at in enumerate(ats):
+            dst[0][s, pl.ds(at, size), :] = high[i * size : (i + 1) * size]
+            dst[1][s, pl.ds(at, size), :] = low[i * size : (i + 1) * size]
+
+
+def forward_stage(first, count, chunks, *rest):
     step = count // chunks
-    size = step * rows
 
     def chunk(c, carry):
-        start = c * step
-        at = pl.multiple_of(start * rows, rows)
-        highs = [src[0][pl.ds(at + o * rows, size), :] for o in range(3)]
-        lows = [src[1][pl.ds(at + o * rows, size), :] for o in range(3)]
-        left = jnp.concatenate(highs + lows + highs, axis=1)
-        for s in range(shots):
-            wh, wl = weights[0][s], weights[1][s]
-            right = jnp.concatenate([wh, wh, wl], axis=0)
-            acc = jnp.dot(left, right, preferred_element_type=F32)
-            light = jnp.concatenate(
-                [
-                    jnp.broadcast_to(light_ref[start + light_at + j, s : s + 1, :], (rows, W))
-                    for j in range(step)
-                ],
-                axis=0,
-            )
-            high, low = split(acc * light)
-            dst[0][s, pl.ds(at, size), :] = high
-            dst[1][s, pl.ds(at, size), :] = low
+        forward_blocks([first + c * step], step, *rest)
         return carry
 
     lax.fori_loop(0, chunks, chunk, 0)
@@ -154,7 +163,8 @@
 
 def kernel(
     n, nb, rows, shots,
-    probes, illum, damp, wav, basis, r_out,
+    probes_in, illum_in, damp_in, wav_in, basis, r_out,
+    probes, illum, damp, wav, in_sems,
     p_left, p_right, l_left, l_right, d_left, d_right,
     xh, xl, rh, rl, yh, yl, zh, zl, fh, fl, ah, al,
     light, damps, g_own, g_all, halo_send, halo_recv, g_send, g_recv,
@@ -162,6 +172,15 @@
     me = lax.axis_index("mp")
     cells = nb * W
 
+    loads = [
+        pltpu.make_async_copy(src, dst, in_sems.at[i])
+        for i, (src, dst) in enumerate(
+            ((wav_in, wav), (probes_in, probes), (illum_in, illum), (damp_in, damp))
+        )
+    ]
+    for load in loads:
+        load.start()
+
     barrier = pltpu.get_barrier_semaphore()
 
     def greet(d, carry):
@@ -172,42 +191,7 @@
 
     lax.fori_loop(1, n, greet, 0)
 
-    def put(b, value):
-        high, low = split(value)
-        xh[b * rows : (b + 1) * rows, :] = high
-        xl[b * rows : (b + 1) * rows, :] = low
-
-    for b in range(nb):
-        put(b + 4, probes[:, b * W : (b + 1) * W])
-        light[b + 3] = illum[:, b * W : (b + 1) * W]
-        damps[b + 2] = damp[:, b * W : (b + 1) * W]
-
-    pl.semaphore_wait(barrier, n - 1)
-
-    def halo(src, depth, to_right, dst, slot):
-        at = pl.ds(cells - depth * W, depth * W) if to_right else pl.ds(0, depth * W)
-        peer = lax.rem(me + 1, n) if to_right else lax.rem(me + n - 1, n)
-        return pltpu.make_async_remote_copy(
-            src_ref=src.at[:, at], dst_ref=dst,
-            send_sem=halo_send.at[slot], recv_sem=halo_recv.at[slot],
-            device_id={"mp": peer}, device_id_type=MESH,
-        )
-
-    rightward = [halo(probes, 4, True, p_left, 0), halo(illum, 3, True, l_left, 1),
-                 halo(damp, 2, True, d_left, 2)]
-    leftward = [halo(probes, 4, False, p_right, 3), halo(illum, 3, False, l_right, 4),
-                halo(damp, 2, False, d_right, 5)]
-
-    @pl.when(me < n - 1)
-    def _():
-        for copy in rightward:
-            copy.start()
-
-    @pl.when(me > 0)
-    def _():
-        for copy in leftward:
-            copy.start()
-
+    loads[0].wait()
     taps = wav[...]
     halves = jnp.concatenate([taps[:, :W], taps[:, W : 2 * W]], axis=0)
     turn = jnp.where(iota((W, W), 0) + iota((W, W), 1) == W - 1, 1.0, 0.0)
@@ -220,6 +204,47 @@
         store_band(taps[s : s + 1, : 2 * W], final[s : s + 1], fh, fl, s)
         store_band(back[s : s + 1], taps[s : s + 1, 0:1], ah, al, s)
 
+    pl.semaphore_wait(barrier, n - 1)
+
+    def halo(src, depth, to_right, dst, slot):
+        at = pl.ds(cells - depth * W, depth * W) if to_right else pl.ds(0, depth * W)
+        peer = lax.rem(me + 1, n) if to_right else lax.rem(me + n - 1, n)
+        return pltpu.make_async_remote_copy(
+            src_ref=src.at[:, at], dst_ref=dst,
+            send_sem=halo_send.at[slot], recv_sem=halo_recv.at[slot],
+            device_id={"mp": peer}, device_id_type=MESH,
+        )
+
+    rightward = [halo(probes_in, 4, True, p_left, 0), halo(illum_in, 3, True, l_left, 1),
+                 halo(damp_in, 2, True, d_left, 2)]
+    leftward = [halo(probes_in, 4, False, p_right, 3), halo(illum_in, 3, False, l_right, 4),
+                halo(damp_in, 2, False, d_right, 5)]
+
+    @pl.when(me < n - 1)
+    def _():
+        for copy in rightward:
+            copy.start()
+
+    @pl.when(me > 0)
+    def _():
+        for copy in leftward:
+            copy.start()
+
+    def put(b, value):
+        high, low = split(value)
+        xh[b * rows : (b + 1) * rows, :] = high
+        xl[b * rows : (b + 1) * rows, :] = low
+
+    for load in loads[1:]:
+        load.wait()
+    for b in range(nb):
+        put(b + 4, probes[:, b * W : (b + 1) * W])
+        light[b + 3] = illum[:, b * W : (b + 1) * W]
+        damps[b + 2] = damp[:, b * W : (b + 1) * W]
+
+    forward = (rows, (xh, xl), (fh, fl), (rh, rl), light, 0, shots)
+    forward_stage(4, nb - 2, 2, *forward)
+
     @pl.when(me > 0)
     def _():
         for copy in rightward:
@@ -282,7 +307,7 @@
         lax.fori_loop(1, n, arrive, 0)
         return unpack(jnp.sum(g_all[k], axis=0)) / (n * cells)
 
-    forward_stage(nb + 6, 2, rows, (xh, xl), (fh, fl), (rh, rl), light, 0, shots)
+    forward_blocks([0, nb + 2], 4, *forward)
     adjoint_stage(nb + 4, 2, rows, (rh, rl), (ah, al), (yh, yl), (xh, xl), damps, 0, shots)
 
     @pl.when(me == 0)
@@ -296,7 +321,7 @@
             ref[(nb + 2) * rows :, :] = jnp.zeros((2 * rows, W), BF16)
 
     send_gram(0, gram_of(yh, yl, 2 * rows, nb, rows))
-    forward_stage(nb + 2, 2, rows, (yh, yl), (fh, fl), (rh, rl), light, 2, shots)
+    forward_stage(0, nb + 2, 2, rows, (yh, yl), (fh, fl), (rh, rl), light, 2, shots)
     adjoint_stage(nb, 2, rows, (rh, rl), (ah, al), (zh, zl), (yh, yl), damps, 2, shots)
     send_gram(1, gram_of(zh, zl, 0, nb, rows))
 
@@ -349,6 +374,8 @@
     damping = damping.reshape(1, cells)
     vmem = pltpu.VMEM
     scratch = [
+        vmem((rows, cells), F32), vmem((shots, cells), F32), vmem((1, cells), F32),
+        vmem(wavelets.shape, F32), pltpu.SemaphoreType.DMA((4,)),
         vmem((rows, 4 * W), F32), vmem((rows, 4 * W), F32),
         vmem((shots, 3 * W), F32), vmem((shots, 3 * W), F32),
         vmem((1, 2 * W), F32), vmem((1, 2 * W), F32),
@@ -370,11 +397,11 @@
             jax.ShapeDtypeStruct((rows, cells), F32),
             jax.ShapeDtypeStruct((rows, rows), F32),
         ),
-        in_specs=[pl.BlockSpec(memory_space=vmem)] * 4,
+        in_specs=[pl.BlockSpec(memory_space=pltpu.HBM)] * 4,
         out_specs=(pl.BlockSpec(memory_space=vmem), pl.BlockSpec(memory_space=vmem)),
         scratch_shapes=scratch,
         compiler_params=pltpu.CompilerParams(
-            collective_id=0, has_side_effects=True, vmem_limit_bytes=48 * 2**20
+            collective_id=0, has_side_effects=True, vmem_limit_bytes=60 * 2**20
         ),
     )(probes, illumination, damping, wavelets)
 

time: 49.9 us -> 44.5 us (0.89)
  Pallas kernels: 43.8 us -> 40.8 us
  local copies, waits for them, and re-layouts: 5.16 us -> 2.88 us
    pallas_call x1, Pallas kernels: 43.8 us -> 40.8 us  [per_device(): pl.pallas_call(functools.partial(kernel, n, nb, rows, shots), out_shape=(...]
    unnamed x10 -> x4, local copies, waits for them, and re-layouts: 5.16 us -> 2.88 us
where the time goes in v1:
time: 44.5 us; the launch traced here: 44.3 us
  Pallas kernels  40.8 us (92%)
  local copies, waits for them, and re-layouts  2.88 us (6%)
  between operations  0.65 us (1%)
    pallas_call x1, Pallas kernels, per_device(): pl.pallas_call(functools.partial(kernel, n, nb, rows, shots), out_shape=(...  40.8 us
    unnamed x4, local copies, waits for them, and re-layouts  2.88 us

profile of v1, /device:TPU:0, one launch (start us, length us, event | category | flops | bytes accessed | tf_op | source)
XLA Modules:
  0.0 44.3 jit_solution(11256462038096798063)
XLA Ops:
  0.6 40.8 %shard_map.59 = (f32[32,8192]{1,0:T(8,128)}, f32[32,32]{1,0:T(8,128)}) custom-call(f32[32,8192]{1,0:T(8,128)} %probes_in.1, f32[4,8192]{1,0:T(4,128)} %illum_in.1, f32[1,8192]{1,0:T(1,128)} %bitcast.1, f32[4,513]{1,0:T(4,128)} %wav_in.1), custom_call_target="tpu_custom_call" | custom-call | tf_op jit(solution)/shard_map/pallas_call | solution.py:394
  41.4 0.0 copy-start
  41.4 2.3 %copy.8 = f32[32,8192]{1,0:T(8,128)} copy(f32[32,8192]{1,0:T(8,128)} %get-tuple-element.4) | data formatting | bytes 2097152
  43.7 0.0 copy-done
  43.7 0.6 %copy.9 = f32[32,32]{1,0:T(8,128)} copy(f32[32,32]{1,0:T(8,128)S(1)} %copy-done) | data formatting | bytes 8192
Async XLA Ops:
  41.4 2.3 %copy-start = (f32[32,32]{1,0:T(8,128)S(1)}, f32[32,32]{1,0:T(8,128)}, u32[]{:S(2)}) copy-start(f32[32,32]{1,0:T(8,128)} %get-tuple-element.5) | copy-start | bytes 12292

commit v2 on v1

--- a/solution.py
+++ b/solution.py
@@ -135,15 +135,18 @@
     def chunk(c, carry):
         start = c * step
         at = pl.multiple_of(start * rows, rows)
-        acc = None
+        left, right = [], []
         for s in range(shots):
             highs = [src[0][s, pl.ds(at + o * rows, size), :] for o in range(3)]
             lows = [src[1][s, pl.ds(at + o * rows, size), :] for o in range(3)]
             wh, wl = weights[0][s], weights[1][s]
-            left = jnp.concatenate(highs + lows + highs, axis=1)
-            right = jnp.concatenate([wh, wh, wl], axis=0)
-            term = jnp.dot(left, right, preferred_element_type=F32)
-            acc = term if acc is None else acc + term
+            left += highs + lows + highs
+            right += [wh, wh, wl]
+        acc = jnp.dot(
+            jnp.concatenate(left, axis=1),
+            jnp.concatenate(right, axis=0),
+            preferred_element_type=F32,
+        )
         own = pl.ds(at + 2 * rows, size)
         value = same[0][own, :].astype(F32) + same[1][own, :].astype(F32)
         damp = jnp.concatenate(

time: 44.5 us -> 44.5 us (level)
  no operation moved by 1% of the time
where the time goes in v2:
time: 44.5 us; the launch traced here: 44.3 us
  Pallas kernels  40.8 us (92%)
  local copies, waits for them, and re-layouts  2.88 us (6%)
  between operations  0.65 us (1%)
    pallas_call x1, Pallas kernels, per_device(): pl.pallas_call(functools.partial(kernel, n, nb, rows, shots), out_shape=(...  40.8 us
    unnamed x4, local copies, waits for them, and re-layouts  2.88 us

profile of v2, /device:TPU:0, one launch (start us, length us, event | category | flops | bytes accessed | tf_op | source)
XLA Modules:
  0.0 44.3 jit_solution(4890336621816456493)
XLA Ops:
  0.6 40.8 %shard_map.59 = (f32[32,8192]{1,0:T(8,128)}, f32[32,32]{1,0:T(8,128)}) custom-call(f32[32,8192]{1,0:T(8,128)} %probes_in.1, f32[4,8192]{1,0:T(4,128)} %illum_in.1, f32[1,8192]{1,0:T(1,128)} %bitcast.1, f32[4,513]{1,0:T(4,128)} %wav_in.1), custom_call_target="tpu_custom_call" | custom-call | tf_op jit(solution)/shard_map/pallas_call | solution.py:397
  41.4 0.0 copy-start
  41.4 2.3 %copy.8 = f32[32,8192]{1,0:T(8,128)} copy(f32[32,8192]{1,0:T(8,128)} %get-tuple-element.4) | data formatting | bytes 2097152
  43.7 0.0 copy-done
  43.7 0.6 %copy.9 = f32[32,32]{1,0:T(8,128)} copy(f32[32,32]{1,0:T(8,128)S(1)} %copy-done) | data formatting | bytes 8192
Async XLA Ops:
  41.4 2.3 %copy-start = (f32[32,32]{1,0:T(8,128)S(1)}, f32[32,32]{1,0:T(8,128)}, u32[]{:S(2)}) copy-start(f32[32,32]{1,0:T(8,128)} %get-tuple-element.5) | copy-start | bytes 12292
